TPU v7x, 512 devices: a whole 4x4x16 slice. The times are simulated.
512 devices in a mesh: trc: 32 (over z_hi, y, x), lev: 16 (over z_lo, core).
Axes of the slice: x: 4, y: 4, z: 16 (z_hi: 2, z_lo: 8; z = z_hi * 8 + z_lo), core: 2. Of those that a mesh axis runs over, the one named last changes fastest.
Arguments:
- tracers: float32 [64, 256, 4, 32, 128], P('lev', 'trc'), may hold values from -6 to 6
- air_mass: float32 [64, 32, 128], P('lev'), may hold values from 2 to 3
- mass_flux: float32 [3, 64, 32, 128], P(None, 'lev', 'trc'), may hold values from -0.3 to 0.3
- chem_inverse: bfloat16 [4, 256, 256], replicated, as said below
- chem_source: float32 [4, 256], replicated, may hold values from -3 to 3
- reaction_set: int32 [64, 32, 128], P('lev', 'trc'), may hold values from 0 to 3
- chem_steps: int32 [64, 32, 128], P('lev', 'trc'), may hold values from 1 to 6
Outputs:
- tracers_out: float32 [64, 256, 4, 32, 128], P('lev', 'trc')
Inputs may be any that keep to these rules, and one draw needn't show every extreme that they name: `chem_inverse`: the diagonal lies in 0.3 to 0.8, every other entry is small.
All inputs are finite; a program needn't handle non-finite values.
Results may differ from a plain program's by a relative error of at most 0.0016.
Values sent between devices are 32-bit elements; how exact they have to be, the bound alone decides.
A program may use at most 64 MiB of HBM per device.

v0:
```python
import jax
import jax.numpy as jnp
from jax import lax
from jax.sharding import PartitionSpec as P

NSTEP = 6


def extended(value, sides, width):
    for axis, dim in sides:
        size, length = (lax.axis_size(axis), value.shape[dim])
        up = [(i, (i + 1) % size) for i in range(size - 1)]
        down = [(j, i) for i, j in up]
        last = lax.slice_in_dim(value, length - width, length, axis=dim)
        leading = lax.slice_in_dim(value, 0, width, axis=dim)
        before = lax.ppermute(last, axis, up)
        after = lax.ppermute(leading, axis, down)
        value = jnp.concatenate([before, value, after], axis=dim)
    return value


def shift_down(values, sweep_axis):
    length = values.shape[sweep_axis]
    filler = jnp.zeros_like(lax.slice_in_dim(values, 0, 1, axis=sweep_axis))
    return jnp.concatenate(
        [filler, lax.slice_in_dim(values, 0, length - 1, axis=sweep_axis)], axis=sweep_axis
    )


def shift_up(values, sweep_axis):
    length = values.shape[sweep_axis]
    filler = jnp.zeros_like(lax.slice_in_dim(values, 0, 1, axis=sweep_axis))
    return jnp.concatenate(
        [lax.slice_in_dim(values, 1, length, axis=sweep_axis), filler], axis=sweep_axis
    )


def close_wall(fluxes, sweep_axis):
    places = lax.broadcasted_iota(jnp.int32, fluxes.shape, sweep_axis)
    return jnp.where(places < fluxes.shape[sweep_axis] - 1, fluxes, jnp.float32(0.0))


def piece_right(mixing, moment, across, beyond, airmass, fluxes):
    carried = jnp.maximum(fluxes, 0.0)
    fraction = carried / jnp.maximum(airmass, 0.5)
    return (carried, mixing + moment * (1.0 - fraction), fraction * moment, across, beyond)


def piece_left(mixing, moment, across, beyond, airmass, fluxes):
    carried = jnp.maximum(-fluxes, 0.0)
    fraction = carried / jnp.maximum(airmass, 0.5)
    return (carried, mixing - moment * (1.0 - fraction), fraction * moment, across, beyond)


def compose(
    mixing, moment, across, beyond, airmass, upper_flux, lower_flux, incoming_left, incoming_right
):
    frac_right = jnp.maximum(upper_flux, 0.0) / airmass
    frac_left = jnp.maximum(-lower_flux, 0.0) / airmass
    remain = 1.0 - frac_left - frac_right
    centre = 0.5 * (frac_left - frac_right)
    remain_mean = mixing + 2.0 * moment * centre
    remain_slope = remain * moment
    remain_air = airmass * remain
    mass_left, mean_left, slope_left, across_left, beyond_left = incoming_left
    mass_right, mean_right, slope_right, across_right, beyond_right = incoming_right
    new_air = mass_left + remain_air + mass_right
    share_left = mass_left / new_air
    share_kept = remain_air / new_air
    share_right = mass_right / new_air
    centre_left = -0.5 + 0.5 * share_left
    centre_kept = -0.5 + share_left + 0.5 * share_kept
    centre_right = 0.5 - 0.5 * share_right
    new_mixing = share_left * mean_left + share_kept * remain_mean + share_right * mean_right
    first_moment = share_left * (centre_left * mean_left + share_left * slope_left / 6.0)
    first_moment = first_moment + share_kept * (
        centre_kept * remain_mean + share_kept * remain_slope / 6.0
    )
    first_moment = first_moment + share_right * (
        centre_right * mean_right + share_right * slope_right / 6.0
    )
    new_across = share_left * across_left + share_kept * across + share_right * across_right
    new_beyond = share_left * beyond_left + share_kept * beyond + share_right * beyond_right
    return (new_mixing, 6.0 * first_moment, new_across, new_beyond, new_air)


def advect_sweep(mixing, moment, across, beyond, airmass, fluxes, sweep_axis):
    lower_flux = shift_down(fluxes, sweep_axis)
    lower_cells = [
        shift_down(values, sweep_axis) for values in (mixing, moment, across, beyond, airmass)
    ]
    upper_cells = [
        shift_up(values, sweep_axis) for values in (mixing, moment, across, beyond, airmass)
    ]
    incoming_left = piece_right(*lower_cells, lower_flux)
    incoming_right = piece_left(*upper_cells, fluxes)
    return compose(
        mixing, moment, across, beyond, airmass, fluxes, lower_flux, incoming_left, incoming_right
    )


def on_device(tracers, air_mass, mass_flux, chem_inverse, chem_source, reaction_set, chem_steps):
    levels_here = tracers.shape[0]
    width = tracers.shape[1]
    airmass = air_mass[:, None]
    mixing = tracers[:, :, 0]
    slope_x = tracers[:, :, 1]
    slope_y = tracers[:, :, 2]
    slope_z = tracers[:, :, 3]
    gathered = lax.all_gather(mass_flux, "trc", axis=2, tiled=True)
    flux_x = gathered[0]
    flux_x = close_wall(flux_x[:, None], 3)
    mixing, slope_x, slope_y, slope_z, air_now = advect_sweep(
        mixing, slope_x, slope_y, slope_z, airmass, flux_x, 3
    )
    flux_y = gathered[1]
    flux_y = close_wall(flux_y[:, None], 2)
    mixing, slope_y, slope_x, slope_z, air_now = advect_sweep(
        mixing, slope_y, slope_x, slope_z, air_now, flux_y, 2
    )
    flux_z = gathered[2]
    flux_z = flux_z[:, None]
    level_index = lax.axis_index("lev") * levels_here + lax.broadcasted_iota(
        jnp.int32, flux_z.shape, 0
    )
    all_levels = levels_here * lax.axis_size("lev")
    flux_z = jnp.where(level_index < all_levels - 1, flux_z, jnp.float32(0.0))
    stacked = jnp.concatenate([mixing, slope_z, slope_x, slope_y, air_now, flux_z], 1)
    padded = extended(stacked, (("lev", 0),), 1)
    near_mix = padded[:, :width]
    near_slope = padded[:, width : 2 * width]
    near_across = padded[:, 2 * width : 3 * width]
    near_beyond = padded[:, 3 * width : 4 * width]
    near_air = padded[:, 4 * width : 4 * width + 1]
    near_flux = padded[:, 4 * width + 1 :]
    lower_flux = near_flux[:levels_here]
    incoming_left = piece_right(
        near_mix[:levels_here],
        near_slope[:levels_here],
        near_across[:levels_here],
        near_beyond[:levels_here],
        near_air[:levels_here],
        near_flux[:levels_here],
    )
    incoming_right = piece_left(
        near_mix[2:],
        near_slope[2:],
        near_across[2:],
        near_beyond[2:],
        near_air[2:],
        near_flux[1 : levels_here + 1],
    )
    mixing, slope_z, slope_x, slope_y, air_now = compose(
        mixing,
        slope_z,
        slope_x,
        slope_y,
        air_now,
        flux_z,
        lower_flux,
        incoming_left,
        incoming_right,
    )
    cells = lax.all_to_all(mixing, "trc", split_axis=2, concat_axis=1, tiled=True)
    row_count = cells.shape[2]
    columns = cells.reshape(levels_here, cells.shape[1], row_count * cells.shape[3])
    set_ids = reaction_set.reshape(levels_here, -1)
    counts = chem_steps.reshape(levels_here, -1)
    select = (
        set_ids[:, None, :] == jnp.arange(chem_inverse.shape[0], dtype=jnp.int32)[None, :, None]
    ).astype(jnp.float32)
    for substep in range(NSTEP):
        rounded = columns.astype(jnp.bfloat16)
        product = jnp.einsum(
            "rts,lsc->lrtc", chem_inverse, rounded, preferred_element_type=jnp.float32
        )
        product = product + chem_source[None, :, :, None]
        updated = jnp.sum(select[:, :, None, :] * product, 1)
        columns = jnp.where(substep < counts[:, None, :], updated, columns)
    finished = lax.all_to_all(
        columns.reshape(cells.shape), "trc", split_axis=1, concat_axis=2, tiled=True
    )
    return jnp.stack([finished, slope_x, slope_y, slope_z], 2)


def solution(mesh):
    return jax.shard_map(
        on_device,
        mesh=mesh,
        in_specs=(
            P("lev", "trc", None, None, None),
            P("lev", None, None),
            P(None, "lev", "trc", None),
            P(),
            P(),
            P("lev", "trc", None),
            P("lev", "trc", None),
        ),
        out_specs=P("lev", "trc", None, None, None),
        check_vma=False,
    )
```

profile of v0, /device:TPU:32, one launch (start us, length us, event | category | flops | bytes accessed | tf_op | source)
XLA Modules:
  0.0 288.0 jit_solution(9834513186752206433)
XLA Ops:
  1.2 163.8 %all_gather.3 = f32[3,4,32,128]{3,1,0,2:T(4,128)S(1)} all-gather(f32[3,4,1,128]{3,1,0,2:T(4,128)} %bitcast.274), channel_id=1, replica_groups=mesh['trc'=32,'lev'=16] {'trc'}, dimensions={2}, use_global_device_ids=true | all-gather | bytes 202752 | tf_op jit(solution)/shard_map/all_gather | solution.py:110
  170.7 1.7 broadcast_multiply_fusion.1
  172.5 2.5 multiply_add_fusion.10
  175.5 1.7 multiply_add_fusion.7
  177.2 1.7 broadcast_multiply_fusion
  178.9 4.5 %concatenate.107 = f32[4,34,32,128]{3,1,2,0:T(8,128)S(1)} concatenate(f32[4,8,32,128]{3,1,2,0:T(8,128)} %get-tuple-element.84, f32[4,8,32,128]{3,1,2,0:T(8,128)} %get-tuple-element.85, f32[4,8,32,128]{3,1,2,0:T(8,128)} %get-tuple-element.89, f32[4,8,32,128]{3,1,2,0:T(8,128)} %get-tuple-element.21, f32[4,1,32,128]{3,1,2,0:T(1,128)S(1)} %get-tuple-element.25, ...), dimensions={1} | concatenate | bytes 4456448 | tf_op jit(solution)/shard_map/concatenate | solution.py:128
  183.6 1.9 collective-permute-start.1
  185.7 2.6 collective-permute-start
  188.3 4.3 %collective-permute-done.1 = f32[1,34,32,128]{3,2,1,0:T(8,128)S(1)} collective-permute-done((f32[1,34,32,128]{3,2,1,0:T(8,128)S(1)}, f32[1,34,32,128]{3,2,1,0:T(8,128)S(1)}, u32[]{:S(2)}, u32[]{:S(2)}) %collective-permute-start.1) | collective-permute-done | bytes 557088 | tf_op jit(solution)/shard_map/ppermute | solution.py:17
  192.9 3.6 %collective-permute-done = f32[1,34,32,128]{3,2,1,0:T(8,128)S(1)} collective-permute-done((f32[1,34,32,128]{3,2,1,0:T(8,128)S(1)}, f32[1,34,32,128]{3,2,1,0:T(8,128)S(1)}, u32[]{:S(2)}, u32[]{:S(2)}) %collective-permute-start) | collective-permute-done | bytes 557088 | tf_op jit(solution)/shard_map/ppermute | solution.py:16
  201.3 4.8 %all-to-all-start = ((f32[4,8,32,128]{3,1,0,2:T(8,128)}), f32[4,8,32,128]{3,1,0,2:T(8,128)}, u32[]{:S(2)}, u32[]{:S(2)}) async-start(f32[4,8,32,128]{3,1,0,2:T(8,128)} %copy.92), calls=%async_computation | async-start | bytes 1048576 | tf_op jit(solution)/shard_map/all_to_all | solution.py:164
  206.2 34.8 %all-to-all-done = f32[4,8,32,128]{3,1,0,2:T(8,128)} async-done(((f32[4,8,32,128]{3,1,0,2:T(8,128)}), f32[4,8,32,128]{3,1,0,2:T(8,128)}, u32[]{:S(2)}, u32[]{:S(2)}) %all-to-all-start) | async-done | bytes 524320 | tf_op jit(solution)/shard_map/all_to_all | solution.py:164
  240.9 1.9 copy.149
  242.8 2.0 copy.96
  244.8 1.8 copy.148
  246.6 1.8 copy.94
  248.4 1.5 fusion.5
  254.6 2.0 copy.97
  256.7 4.6 %all-to-all-start.1 = ((f32[4,256,1,128]{3,0,2,1:T(4,128)}), f32[4,256,1,128]{3,0,2,1:T(4,128)}, u32[]{:S(2)}, u32[]{:S(2)}) async-start(f32[4,256,1,128]{3,0,2,1:T(4,128)} %copy.97), calls=%async_computation.1 | async-start | bytes 1048576 | tf_op jit(solution)/shard_map/all_to_all | solution.py:180
  261.4 2.9 fusion.12
  264.4 1.5 multiply_bitcast_fusion
  265.9 17.9 %all-to-all-done.1 = f32[4,256,1,128]{3,0,2,1:T(4,128)} async-done(((f32[4,256,1,128]{3,0,2,1:T(4,128)}), f32[4,256,1,128]{3,0,2,1:T(4,128)}, u32[]{:S(2)}, u32[]{:S(2)}) %all-to-all-start.1) | async-done | bytes 524320 | tf_op jit(solution)/shard_map/all_to_all | solution.py:180
  284.8 1.6 pad_maximum_fusion
  286.4 1.7 copy.99
  (112 shorter events, 18.3 us)
Async XLA Ops:
  0.0 248.4 %copy-start = (bf16[4,256,256]{2,1,0:T(8,128)(2,1)S(1)}, bf16[4,256,256]{2,1,0:T(8,128)(2,1)}, u32[]{:S(2)}) copy-start(bf16[4,256,256]{2,1,0:T(8,128)(2,1)} %param.10) | copy-start | bytes 1572868
  0.0 166.4 %copy-start.11 = (f32[4,32,128]{2,1,0:T(8,128)S(1)}, f32[4,32,128]{2,1,0:T(8,128)}, u32[]{:S(2)}) copy-start(f32[4,32,128]{2,1,0:T(8,128)} %param.8) | copy-start | bytes 196612
  165.2 3.3 %copy-start.10 = (f32[4,8,4,32,128]{4,3,2,1,0:T(8,128)S(1)}, f32[4,8,4,32,128]{4,3,2,1,0:T(8,128)}, u32[]{:S(2)}) copy-start(f32[4,8,4,32,128]{4,3,2,1,0:T(8,128)} %param.7) | copy-start | bytes 6291460
  183.6 9.0 %collective-permute-start.1 = (f32[1,34,32,128]{3,2,1,0:T(8,128)S(1)}, f32[1,34,32,128]{3,2,1,0:T(8,128)S(1)}, u32[]{:S(2)}, u32[]{:S(2)}) collective-permute-start(f32[1,34,32,128]{3,2,1,0:T(8,128)S(1)} %copy.90), channel_id=1, source_target_pairs={{1,0},{2,1},{3,2},{4,3},{5,4},{6,5},{7,6},{8,7},{9,8},{10,9},{11,1... | collective-permute-start | bytes 1671176 | tf_op jit(solution)/shard_map/ppermute | solution.py:17
  185.7 10.9 %collective-permute-start = (f32[1,34,32,128]{3,2,1,0:T(8,128)S(1)}, f32[1,34,32,128]{3,2,1,0:T(8,128)S(1)}, u32[]{:S(2)}, u32[]{:S(2)}) collective-permute-start(f32[1,34,32,128]{3,2,1,0:T(8,128)S(1)} %copy.88), channel_id=1, source_target_pairs={{0,1},{1,2},{2,3},{3,4},{4,5},{5,6},{6,7},{7,8},{8,9},{9,10},{10,1... | collective-permute-start | bytes 1671176 | tf_op jit(solution)/shard_map/ppermute | solution.py:16
  192.9 7.1 %copy-start.1 = (f32[1,34,32,128]{3,1,2,0:T(8,128)}, f32[1,34,32,128]{3,1,2,0:T(8,128)S(1)}, u32[]{:S(2)}) copy-start(f32[1,34,32,128]{3,1,2,0:T(8,128)S(1)} %copy.91) | copy-start | bytes 1671172
  196.9 3.1 %copy-start.3 = (f32[1,34,32,128]{3,1,2,0:T(8,128)}, f32[1,34,32,128]{3,1,2,0:T(8,128)S(1)}, u32[]{:S(2)}) copy-start(f32[1,34,32,128]{3,1,2,0:T(8,128)S(1)} %copy.89) | copy-start | bytes 1671172
  196.9 3.1 %copy-start.5 = (f32[4,8,32,128]{3,1,2,0:T(8,128)S(1)}, f32[4,8,32,128]{3,1,2,0:T(8,128)}, u32[]{:S(2)}) copy-start(f32[4,8,32,128]{3,1,2,0:T(8,128)} %get-tuple-element.84) | copy-start | bytes 1572868
  196.9 3.1 %copy-start.7 = (f32[4,8,32,128]{3,1,2,0:T(8,128)S(1)}, f32[4,8,32,128]{3,1,2,0:T(8,128)}, u32[]{:S(2)}) copy-start(f32[4,8,32,128]{3,1,2,0:T(8,128)} %get-tuple-element.85) | copy-start | bytes 1572868
  200.4 5.7 %copy-start.24 = (s32[4,1,128]{2,1,0:T(1,128)S(1)}, s32[4,1,128]{2,1,0:T(1,128)}, u32[]{:S(2)}) copy-start(s32[4,1,128]{2,1,0:T(1,128)} %param.13) | copy-start | bytes 6148
  200.4 5.7 %copy-start.25 = (s32[4,1,128]{2,1,0:T(1,128)S(1)}, s32[4,1,128]{2,1,0:T(1,128)}, u32[]{:S(2)}) copy-start(s32[4,1,128]{2,1,0:T(1,128)} %param.12) | copy-start | bytes 6148
  201.3 47.1 %copy-start.26 = (f32[4,256]{1,0:T(4,128)S(1)}, f32[4,256]{1,0:T(4,128)}, u32[]{:S(2)}) copy-start(f32[4,256]{1,0:T(4,128)} %param.11) | copy-start | bytes 12292
  201.3 39.6 %all-to-all-start = ((f32[4,8,32,128]{3,1,0,2:T(8,128)}), f32[4,8,32,128]{3,1,0,2:T(8,128)}, u32[]{:S(2)}, u32[]{:S(2)}) async-start(f32[4,8,32,128]{3,1,0,2:T(8,128)} %copy.92), calls=%async_computation | async-start | bytes 1048576 | tf_op jit(solution)/shard_map/all_to_all | solution.py:164
  256.7 27.1 %all-to-all-start.1 = ((f32[4,256,1,128]{3,0,2,1:T(4,128)}), f32[4,256,1,128]{3,0,2,1:T(4,128)}, u32[]{:S(2)}, u32[]{:S(2)}) async-start(f32[4,256,1,128]{3,0,2,1:T(4,128)} %copy.97), calls=%async_computation.1 | async-start | bytes 1048576 | tf_op jit(solution)/shard_map/all_to_all | solution.py:180
  261.3 3.0 %copy-start.2 = (f32[1,34,32,128]{3,1,2,0:T(8,128)S(1)}, f32[1,34,32,128]{3,1,2,0:T(8,128)}, u32[]{:S(2)}) copy-start(f32[1,34,32,128]{3,1,2,0:T(8,128)} %copy-done.1) | copy-start | bytes 1671172
  261.3 3.0 %copy-start.4 = (f32[1,34,32,128]{3,1,2,0:T(8,128)S(1)}, f32[1,34,32,128]{3,1,2,0:T(8,128)}, u32[]{:S(2)}) copy-start(f32[1,34,32,128]{3,1,2,0:T(8,128)} %copy-done.3) | copy-start | bytes 1671172
  261.3 3.0 %copy-start.6 = (f32[4,8,32,128]{3,1,2,0:T(8,128)S(1)}, f32[4,8,32,128]{3,1,2,0:T(8,128)}, u32[]{:S(2)}) copy-start(f32[4,8,32,128]{3,1,2,0:T(8,128)} %get-tuple-element.84) | copy-start | bytes 1572868
  261.3 3.0 %copy-start.8 = (f32[4,8,32,128]{3,1,2,0:T(8,128)S(1)}, f32[4,8,32,128]{3,1,2,0:T(8,128)}, u32[]{:S(2)}) copy-start(f32[4,8,32,128]{3,1,2,0:T(8,128)} %get-tuple-element.85) | copy-start | bytes 1572868
  261.3 3.0 %copy-start.14 = (f32[4,1,32,128]{3,1,2,0:T(1,128)S(1)}, f32[4,1,32,128]{3,1,2,0:T(1,128)}, u32[]{:S(2)}) copy-start(f32[4,1,32,128]{3,1,2,0:T(1,128)} %copy-done.13) | copy-start | bytes 196612
  261.3 3.0 %copy-start.16 = (f32[4,1,32,128]{3,1,2,0:T(1,128)S(1)}, f32[4,1,32,128]{3,1,2,0:T(1,128)}, u32[]{:S(2)}) copy-start(f32[4,1,32,128]{3,1,2,0:T(1,128)} %copy-done.15) | copy-start | bytes 196612
  261.4 3.0 %copy-start.18 = (f32[4,1,32,128]{3,1,2,0:T(1,128)S(1)}, f32[4,1,32,128]{3,1,2,0:T(1,128)}, u32[]{:S(2)}) copy-start(f32[4,1,32,128]{3,1,2,0:T(1,128)} %copy-done.17) | copy-start | bytes 196612
  261.4 3.0 %copy-start.19 = (f32[4,1,32,128]{3,1,2,0:T(1,128)S(1)}, f32[4,1,32,128]{3,1,2,0:T(1,128)}, u32[]{:S(2)}) copy-start(f32[4,1,32,128]{3,1,2,0:T(1,128)} %get-tuple-element.8) | copy-start | bytes 196612
  261.4 3.0 %copy-start.20 = (f32[4,1,32,128]{3,1,2,0:T(1,128)S(1)}, f32[4,1,32,128]{3,1,2,0:T(1,128)}, u32[]{:S(2)}) copy-start(f32[4,1,32,128]{3,1,2,0:T(1,128)} %get-tuple-element.58) | copy-start | bytes 196612
  261.4 3.0 %copy-start.21 = (f32[4,1,32,128]{3,1,2,0:T(1,128)S(1)}, f32[4,1,32,128]{3,1,2,0:T(1,128)}, u32[]{:S(2)}) copy-start(f32[4,1,32,128]{3,1,2,0:T(1,128)} %get-tuple-element.13) | copy-start | bytes 196612
  (7 other events, 14.4 us)
where the time goes:
time: 289 us; the launch traced here: 288 us
  blocking collectives  164 us (57%)
  waiting for transfers between devices  60.5 us (21%)
  local copies, waits for them, and re-layouts  22.8 us (8%)
  other arithmetic  22.1 us (8%)
  starting transfers between devices  13.9 us (5%)
  matrix products  4.26 us (1%)
    all_gather x1, blocking collectives, on_device(): gathered = lax.all_gather(mass_flux, 'trc', axis=2, tiled=True)  164 us
    all_to_all x1, waiting for transfers between devices, on_device(): lax.all_to_all(mixing, 'trc', split_axis=2, concat_axis=1, tiled=True)  34.8 us
    all_to_all x1, waiting for transfers between devices, on_device(): lax.all_to_all(columns.reshape(cells.shape), 'trc', split_axis=1, concat_...  17.9 us
    another operation x3, other arithmetic, on_device(): return jnp.stack([finished, slope_x, slope_y, slope_z], 2)  5.9 us
  transfers between devices with their start and end apart: 4, of which 4 were waited for; matrix products, arithmetic and copies ran while one was open for 2% of the time, Pallas kernels for 0%

commit v1 on v0

v1 whole, which is shorter than its diff:
```python
import jax
import jax.numpy as jnp
from jax import lax
from jax.experimental import pallas as pl
from jax.experimental.pallas import tpu as pltpu
from jax.sharding import PartitionSpec as P

MESH = pl.DeviceIdType.MESH
F32 = jnp.float32
LEV, TRC, LAT, LON = 4, 8, 32, 128
HALF = 16
NT, SETS, NSTEP = 256, 4, 6
PACK = 24


def lower_of(value, axis):
    return pltpu.roll(value, 1, axis)


def upper_of(value, axis):
    return pltpu.roll(value, value.shape[axis] - 1, axis)


def coefficients(air_below, air, air_above, lower, upper):
    from_below = jnp.maximum(lower, 0.0)
    from_above = jnp.maximum(-upper, 0.0)
    fraction_below = from_below / jnp.maximum(air_below, 0.5)
    fraction_above = from_above / jnp.maximum(air_above, 0.5)
    inverse = 1.0 / air
    out_up = jnp.maximum(upper, 0.0) * inverse
    out_down = jnp.maximum(-lower, 0.0) * inverse
    remain = 1.0 - out_down - out_up
    kept = air * remain
    new_air = from_below + kept + from_above
    inverse = 1.0 / new_air
    share_l, share_0, share_r = from_below * inverse, kept * inverse, from_above * inverse
    six_l, six_0, six_r = 6.0 * share_l, 6.0 * share_0, 6.0 * share_r
    return (
        new_air,
        (1.0 - fraction_below, out_down - out_up, fraction_above - 1.0, share_l, share_0, share_r),
        (
            six_l * (0.5 * share_l - 0.5),
            six_0 * (share_l + 0.5 * share_0 - 0.5),
            six_r * (0.5 - 0.5 * share_r),
            share_l * share_l * fraction_below,
            share_0 * share_0 * remain,
            share_r * share_r * fraction_above,
        ),
    )


def means(mixing, slope, first):
    (qm, q, qp), (sm, s, sp) = mixing, slope
    return qm + sm * first[0], q + s * first[1], qp + sp * first[2]


def carried(values, first):
    return first[3] * values[0] + first[4] * values[1] + first[5] * values[2]


def new_slope(mean, slope, second):
    total = second[0] * mean[0] + second[1] * mean[1] + second[2] * mean[2]
    return total + (second[3] * slope[0] + second[4] * slope[1] + second[5] * slope[2])


def around(value, axis):
    return lower_of(value, axis), value, upper_of(value, axis)


def kernel(
    tracers, air_mass, fluxes, inverse, source, sets, steps, out,
    raw, air, flux_in, sets_in, steps_in, matrix, source_in, gathered,
    half_x, half_y, half_air, half_flux, half_z,
    coef, coef_z, state, below, above, result,
    send_mid, send_edge, send_row, columns, work, finished, returned,
    local_sem, out_sem, flux_send, flux_recv, halo_send, halo_recv, cell_send, cell_recv, back_send, back_recv,
):
    t, l = lax.axis_index("trc"), lax.axis_index("lev")
    plane, me = lax.div(t, HALF), lax.rem(t, HALF)
    other = 1 - plane
    edge_row = (HALF - 1) * other
    own = pl.multiple_of(t * PACK, 8)
    partner = other * HALF + me

    def device(which_plane, place):
        return {"trc": which_plane * HALF + place, "lev": l}

    def put(src, dst, send, recv, to):
        pltpu.make_async_remote_copy(
            src_ref=src, dst_ref=dst, send_sem=send, recv_sem=recv, device_id=to, device_id_type=MESH
        ).start()

    def settle(ref, sem):
        pltpu.make_async_copy(ref, ref, sem).wait()

    loads = [
        pltpu.make_async_copy(fluxes, flux_in, local_sem.at[0]),
        pltpu.make_async_copy(sets, sets_in, local_sem.at[1]),
        pltpu.make_async_copy(steps, steps_in, local_sem.at[2]),
        pltpu.make_async_copy(air_mass, air, local_sem.at[3]),
        pltpu.make_async_copy(tracers, raw, local_sem.at[4]),
        pltpu.make_async_copy(source, source_in.at[pl.ds(0, SETS)], local_sem.at[5]),
    ] + [
        pltpu.make_async_copy(inverse.at[k], matrix.at[:, pl.ds(k * NT, NT)], local_sem.at[6 + k])
        for k in range(SETS)
    ]
    for load in loads:
        load.start()

    barrier = pltpu.get_barrier_semaphore()
    pl.semaphore_signal(barrier, inc=1, device_id=device(other, me), device_id_type=MESH)

    def greet(k, _):
        pl.semaphore_signal(
            barrier, inc=1, device_id=device(plane, lax.rem(me + k, HALF)), device_id_type=MESH
        )
        return 0

    lax.fori_loop(1, HALF, greet, 0)

    @pl.when(l > 0)
    def _():
        pl.semaphore_signal(barrier, inc=1, device_id={"trc": t, "lev": l - 1}, device_id_type=MESH)

    @pl.when(l < 15)
    def _():
        pl.semaphore_signal(barrier, inc=1, device_id={"trc": t, "lev": l + 1}, device_id_type=MESH)

    for load in loads[:3]:
        load.wait()
    gathered[pl.ds(own, 16), :] = jnp.concatenate(
        [flux_in[...], sets_in[...].astype(F32)], axis=0
    )
    gathered[pl.ds(own + 16, 8), :] = jnp.concatenate(
        [steps_in[...].astype(F32), jnp.zeros((4, LON), F32)], axis=0
    )

    @pl.when(l == 0)
    def _():
        below[...] = jnp.zeros_like(below)

    @pl.when(l == 15)
    def _():
        above[...] = jnp.zeros_like(above)

    pl.semaphore_wait(barrier, HALF + (l > 0).astype(jnp.int32) + (l < 15).astype(jnp.int32))

    mine = gathered.at[pl.ds(own, PACK)]
    put(mine, mine, flux_send.at[0], flux_recv.at[1], device(other, me))

    def share_own(k, _):
        put(mine, mine, flux_send.at[0], flux_recv.at[0], device(plane, lax.rem(me + k, HALF)))
        return 0

    lax.fori_loop(1, HALF, share_own, 0)
    for load in loads[3:5]:
        load.wait()
    settle(gathered.at[pl.ds(0, 15 * PACK)], flux_recv.at[0])

    lane = lax.broadcasted_iota(jnp.int32, (HALF, LON), 1)
    row = lax.broadcasted_iota(jnp.int32, (HALF, LON), 0) + plane * HALF
    first_row = pl.multiple_of(plane * HALF, HALF)
    top_level = 16 * LEV - 1

    def half_coefficients(level, _):
        def flux(direction):
            start = plane * (HALF * PACK) + direction * LEV + level
            return gathered[pl.ds(start, HALF, stride=PACK), :]

        cell_air = air[level, pl.ds(first_row, HALF), :]
        upper = jnp.where(lane < LON - 1, flux(0), 0.0)
        new_air, first, _ = coefficients(
            lower_of(cell_air, 1), cell_air, upper_of(cell_air, 1), lower_of(upper, 1), upper
        )
        for n in range(6):
            half_x[level, n] = first[n]
        upper = jnp.where(row < LAT - 1, flux(1), 0.0)
        lower = jnp.where(row > 0, lower_of(upper, 0), 0.0)
        new_air, first, _ = coefficients(
            lower_of(new_air, 0), new_air, upper_of(new_air, 0), lower, upper
        )
        for n in range(6):
            half_y[level, n] = first[n]
        half_air[level] = new_air
        half_flux[level] = flux(2)
        return 0

    lax.fori_loop(0, LEV, half_coefficients, 0)
    for level in (1, 2):
        _, first, _ = coefficients(
            half_air[level - 1], half_air[level], half_air[level + 1], half_flux[level - 1], half_flux[level]
        )
        for n in range(6):
            half_z[level - 1, n] = first[n]

    mid_rows = send_mid.reshape(HALF * 2 * 2 * TRC, LON)

    def half_tracer(n, _):
        mixing, slope = [], []
        for level in range(LEV):
            q, sx, sy, sz = (raw[level, n, f, pl.ds(first_row, HALF), :] for f in range(4))
            first = [half_x[level, i] for i in range(6)]
            q = carried(means(around(q, 1), around(sx, 1), first), first)
            sy = carried(around(sy, 1), first)
            sz = carried(around(sz, 1), first)
            first = [half_y[level, i] for i in range(6)]
            mixing.append(carried(means(around(q, 0), around(sy, 0), first), first))
            slope.append(carried(around(sz, 0), first))
        for level in (1, 2):
            first = [half_z[level - 1, i] for i in range(6)]
            q = carried(means(mixing[level - 1 : level + 2], slope[level - 1 : level + 2], first), first)
            mid_rows[pl.ds(plane * 16 + (level - 1) * TRC + n, HALF, stride=32), :] = q
        return 0

    lax.fori_loop(0, TRC, half_tracer, 0)
    my_rows = pl.ds(pl.multiple_of(t * TRC, TRC), TRC)

    def spread(first_k, which_plane, start):
        def one(k, _):
            start(which_plane, lax.rem(me + k, HALF))
            return 0

        lax.fori_loop(first_k, HALF, one, 0)

    def send_own_half(which_plane, place):
        @pl.when(place != edge_row)
        def _():
            put(
                send_mid.at[place, plane], columns.at[pl.ds(1, 2), plane, my_rows],
                cell_send.at[0], cell_recv.at[0], device(which_plane, place),
            )

    spread(0, other, send_own_half)
    spread(1, plane, send_own_half)

    theirs = gathered.at[pl.ds(pl.multiple_of(partner * PACK, 8), PACK)]
    settle(theirs, flux_recv.at[1])

    def share_partner(k, _):
        put(theirs, theirs, flux_send.at[0], flux_recv.at[2], device(plane, lax.rem(me + k, HALF)))
        return 0

    lax.fori_loop(1, HALF, share_partner, 0)
    settle(gathered.at[pl.ds(0, 15 * PACK)], flux_recv.at[2])

    lane = lax.broadcasted_iota(jnp.int32, (LAT, LON), 1)
    row = lax.broadcasted_iota(jnp.int32, (LAT, LON), 0)

    def full_coefficients(level, _):
        def flux(direction):
            return gathered[pl.ds(direction * LEV + level, LAT, stride=PACK), :]

        cell_air = air[level]
        upper = jnp.where(lane < LON - 1, flux(0), 0.0)
        new_air, first, second = coefficients(
            lower_of(cell_air, 1), cell_air, upper_of(cell_air, 1), lower_of(upper, 1), upper
        )
        for n in range(6):
            coef[level, n] = first[n]
            coef[level, 6 + n] = second[n]
        upper = jnp.where(row < LAT - 1, flux(1), 0.0)
        new_air, first, second = coefficients(
            lower_of(new_air, 0), new_air, upper_of(new_air, 0), lower_of(upper, 0), upper
        )
        for n in range(6):
            coef[level, 12 + n] = first[n]
            coef[level, 18 + n] = second[n]
        state[level, 4 * TRC] = new_air
        state[level, 4 * TRC + 1] = jnp.where(l * LEV + level < top_level, flux(2), 0.0)
        return 0

    lax.fori_loop(0, LEV, full_coefficients, 0)

    def horizontal(level):
        def tracer(n, _):
            q, sx, sy, sz = (raw[level, n, f] for f in range(4))
            first = [coef[level, i] for i in range(6)]
            second = [coef[level, 6 + i] for i in range(6)]
            slope = around(sx, 1)
            mean = means(around(q, 1), slope, first)
            q, sx = carried(mean, first), new_slope(mean, slope, second)
            sy, sz = carried(around(sy, 1), first), carried(around(sz, 1), first)
            first = [coef[level, 12 + i] for i in range(6)]
            second = [coef[level, 18 + i] for i in range(6)]
            slope = around(sy, 0)
            mean = means(around(q, 0), slope, first)
            state[level, n] = carried(mean, first)
            state[level, TRC + n] = carried(around(sz, 0), first)
            state[level, 2 * TRC + n] = carried(around(sx, 0), first)
            state[level, 3 * TRC + n] = new_slope(mean, slope, second)
            return 0

        lax.fori_loop(0, TRC, tracer, 0)

    horizontal(0)

    @pl.when(l > 0)
    def _():
        put(state.at[0], above, halo_send.at[0], halo_recv.at[0], {"trc": t, "lev": l - 1})

    horizontal(3)

    @pl.when(l < 15)
    def _():
        put(state.at[3], below, halo_send.at[1], halo_recv.at[1], {"trc": t, "lev": l + 1})

    def inner(level, _):
        horizontal(level)
        return 0

    lax.fori_loop(1, 3, inner, 0)

    edge_rows = send_edge.reshape(2 * HALF * 2 * TRC, LON)

    def vertical(level, lower_level, upper_level, keep):
        _, first, second = coefficients(
            lower_level[4 * TRC], state[level, 4 * TRC], upper_level[4 * TRC],
            lower_level[4 * TRC + 1], state[level, 4 * TRC + 1],
        )
        for i in range(6):
            coef_z[i] = first[i]
            coef_z[6 + i] = second[i]

        def tracer(n, _):
            first = [coef_z[i] for i in range(6)]
            second = [coef_z[6 + i] for i in range(6)]

            def three(f):
                return lower_level[f * TRC + n], state[level, f * TRC + n], upper_level[f * TRC + n]

            slope = three(1)
            mean = means(three(0), slope, first)
            result[level, n, 3] = new_slope(mean, slope, second)
            result[level, n, 1] = carried(three(2), first)
            result[level, n, 2] = carried(three(3), first)
            keep(n, carried(mean, first))
            return 0

        lax.fori_loop(0, TRC, tracer, 0)

    def slopes_out(level):
        return pltpu.make_async_copy(
            result.at[level, :, pl.ds(1, 3)], out.at[level, :, pl.ds(1, 3)], out_sem.at[0, level]
        )

    is_low = plane == 0
    for level in (1, 2):

        def keep_mid(n, q, level=level):
            far = jnp.where(is_low, q[HALF:], q[:HALF])
            mid_rows[pl.ds(other * 16 + (level - 1) * TRC + n, HALF, stride=32), :] = far
            near = jnp.where(is_low, q[HALF - 1 : HALF], q[HALF : HALF + 1])
            send_row[level - 1, pl.ds(n, 1), :] = near

        vertical(level, state.at[level - 1], state.at[level + 1], keep_mid)

    def send_other_half(which_plane, place):
        put(
            send_mid.at[place, other], columns.at[pl.ds(1, 2), other, my_rows],
            cell_send.at[0], cell_recv.at[0], device(which_plane, place),
        )

        @pl.when(place == edge_row)
        def _():
            put(
                send_row, columns.at[pl.ds(1, 2), plane, my_rows],
                cell_send.at[0], cell_recv.at[0], device(which_plane, place),
            )

    spread(0, other, send_other_half)
    spread(1, plane, send_other_half)
    columns[pl.ds(1, 2), other, my_rows, :] = send_mid[me, other]
    columns[pl.ds(1, 2), plane, my_rows, :] = jnp.where(
        me == edge_row, send_row[...], send_mid[me, plane]
    )
    slopes_out(1).start()
    slopes_out(2).start()

    def edge_level(which, lower_level, upper_level):
        level = 3 * which

        def keep_edge(n, q):
            for half in range(2):
                edge_rows[pl.ds(which * 256 + half * TRC + n, HALF, stride=16), :] = q[
                    half * HALF : (half + 1) * HALF
                ]

        vertical(level, lower_level, upper_level, keep_edge)

        def send_level(which_plane, place):
            put(
                send_edge.at[which, place], columns.at[level, :, my_rows],
                cell_send.at[1 + which], cell_recv.at[1 + which], device(which_plane, place),
            )

        spread(0, other, send_level)
        spread(1, plane, send_level)
        columns[level, :, my_rows, :] = send_edge[which, me]
        slopes_out(level).start()

    @pl.when(l > 0)
    def _():
        settle(below, halo_recv.at[1])

    edge_level(0, below, state.at[1])

    @pl.when(l < 15)
    def _():
        settle(above, halo_recv.at[0])

    edge_level(1, state.at[2], above)

    for load in loads[5:]:
        load.wait()
    source_in[pl.ds(4, 4), :] = jnp.zeros((4, NT), F32)
    returned_rows = returned.reshape(LEV * 2 * HALF * TRC, LON)

    def assemble(level):
        settle(returned.at[level, :, pl.ds(0, HALF - 1)], back_recv.at[level])

        def tracer(n, _):
            for half in range(2):
                start = level * 256 + half * 128 + n
                result[level, n, 0, pl.ds(half * HALF, HALF), :] = returned_rows[
                    pl.ds(start, HALF, stride=TRC), :
                ]
            return 0

        lax.fori_loop(0, TRC, tracer, 0)
        mixing_out(level).start()

    def mixing_out(level):
        return pltpu.make_async_copy(
            result.at[level, :, 0], out.at[level, :, 0], out_sem.at[1, level]
        )

    my_tracers = pl.ds(pl.multiple_of(plane * 128, 128), 128)

    def chemistry(i, _):
        level = jnp.where(i < 2, i + 1, 3 * (i - 2))

        @pl.when(i == 0)
        def _():
            settle(columns.at[pl.ds(1, 2), :, pl.ds(0, 248)], cell_recv.at[0])

        @pl.when(i == 2)
        def _():
            settle(columns.at[0, :, pl.ds(0, 248)], cell_recv.at[1])

        @pl.when(i == 3)
        def _():
            assemble(1)
            assemble(2)
            settle(columns.at[3, :, pl.ds(0, 248)], cell_recv.at[2])

        def cell_row(offset):
            return jnp.concatenate(
                [gathered[pl.ds((half * HALF + me) * PACK + offset + level, 1), :] for half in range(2)], axis=1
            )

        cell_sets, cell_steps = cell_row(12), cell_row(16)
        masks = [(cell_sets == k).astype(F32) for k in range(SETS)]
        by_set = source_in[...].T
        added = masks[0] * by_set[:, 0:1]
        for k in range(1, SETS):
            added = added + masks[k] * by_set[:, k : k + 1]
        masks = [m.astype(jnp.bfloat16) for m in masks]
        work[0] = jnp.concatenate([columns[level, 0], columns[level, 1]], axis=1)
        work[1] = added

        def step(turn, _):
            now = work[0]
            rounded = now.astype(jnp.bfloat16)
            chosen = jnp.concatenate([rounded * m for m in masks], axis=0)
            product = jnp.dot(matrix[...], chosen, preferred_element_type=F32)
            work[0] = jnp.where(turn.astype(F32) < cell_steps, product + work[1], now)
            return 0

        lax.fori_loop(0, NSTEP, step, 0)
        for half in range(2):
            finished[level, half] = work[0, my_tracers, pl.ds(half * LON, LON)]

        def send_back(which_plane, place):
            put(
                finished.at[level, :, pl.ds(pl.multiple_of(place * TRC, TRC), TRC)], returned.at[level, :, me],
                back_send.at[0], back_recv.at[level], device(which_plane, place),
            )

        spread(1, plane, send_back)
        returned[level, :, me] = finished[level, :, pl.ds(pl.multiple_of(me * TRC, TRC), TRC), :]
        return 0

    lax.fori_loop(0, LEV, chemistry, 0)
    assemble(0)
    assemble(3)

    settle(gathered.at[pl.ds(0, 31 * PACK)], flux_send.at[0])

    @pl.when(l > 0)
    def _():
        settle(above, halo_send.at[0])

    @pl.when(l < 15)
    def _():
        settle(below, halo_send.at[1])

    settle(columns.at[pl.ds(1, 2), :, pl.ds(0, 248)], cell_send.at[0])
    settle(columns.at[0, :, pl.ds(0, 248)], cell_send.at[1])
    settle(columns.at[3, :, pl.ds(0, 248)], cell_send.at[2])
    settle(returned.at[:, :, pl.ds(0, HALF - 1)], back_send.at[0])
    for level in range(LEV):
        slopes_out(level).wait()
        mixing_out(level).wait()


def on_device(tracers, air_mass, mass_flux, chem_inverse, chem_source, reaction_set, chem_steps):
    anywhere = pl.BlockSpec(memory_space=pl.ANY)
    dma, vmem = pltpu.SemaphoreType.DMA, pltpu.VMEM
    return pl.pallas_call(
        kernel,
        name="advect_and_react",
        out_shape=jax.ShapeDtypeStruct(tracers.shape, F32),
        in_specs=[anywhere] * 7,
        out_specs=anywhere,
        scratch_shapes=[
            vmem(tracers.shape, F32),
            vmem((LEV, LAT, LON), F32),
            vmem((12, LON), F32),
            vmem((LEV, LON), jnp.int32),
            vmem((LEV, LON), jnp.int32),
            vmem((NT, SETS * NT), jnp.bfloat16),
            vmem((8, NT), F32),
            vmem((LAT * PACK, LON), F32),
            vmem((LEV, 6, HALF, LON), F32),
            vmem((LEV, 6, HALF, LON), F32),
            vmem((LEV, HALF, LON), F32),
            vmem((LEV, HALF, LON), F32),
            vmem((2, 6, HALF, LON), F32),
            vmem((LEV, 24, LAT, LON), F32),
            vmem((12, LAT, LON), F32),
            vmem((LEV, 4 * TRC + 2, LAT, LON), F32),
            vmem((4 * TRC + 2, LAT, LON), F32),
            vmem((4 * TRC + 2, LAT, LON), F32),
            vmem(tracers.shape, F32),
            vmem((HALF, 2, 2, TRC, LON), F32),
            vmem((2, HALF, 2, TRC, LON), F32),
            vmem((2, TRC, LON), F32),
            vmem((LEV, 2, NT, LON), F32),
            vmem((2, NT, 2 * LON), F32),
            vmem((LEV, 2, NT // 2, LON), F32),
            vmem((LEV, 2, HALF, TRC, LON), F32),
            dma((10,)),
            dma((2, LEV)),
            dma((1,)),
            dma((3,)),
            dma((2,)),
            dma((2,)),
            dma((3,)),
            dma((3,)),
            dma((1,)),
            dma((LEV,)),
        ],
        compiler_params=pltpu.CompilerParams(
            collective_id=0, has_side_effects=True, vmem_limit_bytes=40 * 1024 * 1024
        ),
    )(
        tracers,
        air_mass,
        mass_flux.reshape(12, LON),
        chem_inverse,
        chem_source,
        reaction_set.reshape(LEV, LON),
        chem_steps.reshape(LEV, LON),
    )


def solution(mesh):
    return jax.shard_map(
        on_device,
        mesh=mesh,
        in_specs=(
            P("lev", "trc", None, None, None),
            P("lev", None, None),
            P(None, "lev", "trc", None),
            P(),
            P(),
            P("lev", "trc", None),
            P("lev", "trc", None),
        ),
        out_specs=P("lev", "trc", None, None, None),
        check_vma=False,
    )
```

time: 289 us -> 99.6 us (0.34)
  the two profiles are of different devices: /device:TPU:32 before, /device:TPU:64 now
where the time goes in v1:
time: 99.6 us; the launch traced here: 99.2 us
  Pallas kernels  91.6 us (92%)
  local copies, waits for them, and re-layouts  7.54 us (8%)
    pallas_call x1, Pallas kernels, on_device(): pl.pallas_call(kernel, name='advect_and_react', out_shape=jax.ShapeDtypeS...  91.6 us
    unnamed x15, local copies, waits for them, and re-layouts  7.54 us

profile of v1, /device:TPU:64, one launch (start us, length us, event | category | flops | bytes accessed | tf_op | source)
XLA Modules:
  0.0 99.2 jit_solution(14875926537968312919)
XLA Ops:
  0.0 0.7 pad
  0.7 0.0 copy-start
  0.7 1.6 %copy-done = f32[4,8,4,32,128]{4,3,2,1,0:T(8,128)S(1)} copy-done((f32[4,8,4,32,128]{4,3,2,1,0:T(8,128)S(1)}, f32[4,8,4,32,128]{4,3,2,1,0:T(8,128)}, u32[]{:S(2)}) %copy-start) | copy-done | bytes 2097176
  2.3 0.0 copy-start.1
  2.3 1.0 %copy-done.1 = bf16[4,256,256]{2,1,0:T(8,128)(2,1)S(1)} copy-done((bf16[4,256,256]{2,1,0:T(8,128)(2,1)S(1)}, bf16[4,256,256]{2,1,0:T(8,128)(2,1)}, u32[]{:S(2)}) %copy-start.1) | copy-done | bytes 524312
  3.3 0.0 copy-start.2
  3.3 0.8 copy-done.2
  4.2 0.0 copy-start.3
  4.2 0.7 copy-done.3
  4.9 0.0 copy-start.4
  4.9 0.7 copy-done.4
  5.5 0.0 copy-start.5
  5.5 0.7 copy-done.5
  6.2 91.6 %advect_and_react.1 = f32[4,8,4,32,128]{4,3,2,1,0:T(8,128)S(1)} custom-call(f32[4,8,4,32,128]{4,3,2,1,0:T(8,128)S(1)} %copy-done, f32[4,32,128]{2,1,0:T(8,128)S(1)} %copy-done.2, f32[12,128]{1,0:T(8,128)S(1)} %bitcast.7, bf16[4,256,256]{2,1,0:T(8,128)(2,1)S(1)} %copy-done.1, f32[4,256]{1,0:T(4,128)S(1)} %copy-done.3, s32[4,128]{1,0:T(4,128)S(1)} %bitcast.8, ...), custom_call_target="tpu_custom_call" | custom-call | tf_op jit(solution)/shard_map/advect_and_react/pallas_call | solution.py:519
  97.9 1.3 %copy.13 = f32[4,8,4,32,128]{4,3,2,1,0:T(8,128)} copy(f32[4,8,4,32,128]{4,3,2,1,0:T(8,128)S(1)} %advect_and_react.1) | data formatting | bytes 4194304
  (1 shorter events, 0.0 us)
Async XLA Ops:
  0.7 1.6 %copy-start = (f32[4,8,4,32,128]{4,3,2,1,0:T(8,128)S(1)}, f32[4,8,4,32,128]{4,3,2,1,0:T(8,128)}, u32[]{:S(2)}) copy-start(f32[4,8,4,32,128]{4,3,2,1,0:T(8,128)} %tracers.1) | copy-start | bytes 6291460
  2.3 1.0 %copy-start.1 = (bf16[4,256,256]{2,1,0:T(8,128)(2,1)S(1)}, bf16[4,256,256]{2,1,0:T(8,128)(2,1)}, u32[]{:S(2)}) copy-start(bf16[4,256,256]{2,1,0:T(8,128)(2,1)} %inverse.1) | copy-start | bytes 1572868
  3.3 0.8 copy-start.2
  4.2 0.7 copy-start.3
  4.9 0.7 copy-start.4
  5.5 0.7 copy-start.5

commit v2 on v1

v2 whole, which is shorter than its diff:
```python
import jax
import jax.numpy as jnp
from jax import lax
from jax.experimental import pallas as pl
from jax.experimental.pallas import tpu as pltpu
from jax.sharding import PartitionSpec as P

MESH = pl.DeviceIdType.MESH
F32 = jnp.float32
LEV, TRC, LAT, LON = 4, 8, 32, 128
HALF = 16
NT, SETS, NSTEP = 256, 4, 6
PACK = 32


def lower_of(value, axis):
    return pltpu.roll(value, 1, axis)


def upper_of(value, axis):
    return pltpu.roll(value, value.shape[axis] - 1, axis)


def coefficients(air_below, air, air_above, lower, upper):
    from_below = jnp.maximum(lower, 0.0)
    from_above = jnp.maximum(-upper, 0.0)
    fraction_below = from_below / jnp.maximum(air_below, 0.5)
    fraction_above = from_above / jnp.maximum(air_above, 0.5)
    inverse = 1.0 / air
    out_up = jnp.maximum(upper, 0.0) * inverse
    out_down = jnp.maximum(-lower, 0.0) * inverse
    remain = 1.0 - out_down - out_up
    kept = air * remain
    new_air = from_below + kept + from_above
    inverse = 1.0 / new_air
    share_l, share_0, share_r = from_below * inverse, kept * inverse, from_above * inverse
    six_l, six_0, six_r = 6.0 * share_l, 6.0 * share_0, 6.0 * share_r
    return (
        new_air,
        (1.0 - fraction_below, out_down - out_up, fraction_above - 1.0, share_l, share_0, share_r),
        (
            six_l * (0.5 * share_l - 0.5),
            six_0 * (share_l + 0.5 * share_0 - 0.5),
            six_r * (0.5 - 0.5 * share_r),
            share_l * share_l * fraction_below,
            share_0 * share_0 * remain,
            share_r * share_r * fraction_above,
        ),
    )


def means(mixing, slope, first):
    (qm, q, qp), (sm, s, sp) = mixing, slope
    return qm + sm * first[0], q + s * first[1], qp + sp * first[2]


def carried(values, first):
    return first[3] * values[0] + first[4] * values[1] + first[5] * values[2]


def new_slope(mean, slope, second):
    total = second[0] * mean[0] + second[1] * mean[1] + second[2] * mean[2]
    return total + (second[3] * slope[0] + second[4] * slope[1] + second[5] * slope[2])


def around(value, axis):
    return lower_of(value, axis), value, upper_of(value, axis)


def kernel(
    tracers, air_mass, fluxes, inverse, source, sets, steps, out,
    raw, air, flux_in, sets_in, steps_in, matrix, source_in, gathered, pack_below, pack_above,
    quick_x, quick_y, quick_z, quick_air, quick_flux,
    coef, coef_z, state,
    send_mid, send_edge, send_row, columns, work, finished, returned,
    local_sem, flux_send, flux_recv, halo_send, halo_recv, cell_send, cell_recv, back_send, back_recv,
):
    t, l = lax.axis_index("trc"), lax.axis_index("lev")
    plane, me = lax.div(t, HALF), lax.rem(t, HALF)
    other = 1 - plane
    edge_row = (HALF - 1) * other
    own = pl.multiple_of(t * PACK, PACK)
    partner = other * HALF + me
    has_below, has_above = l > 0, l < 15

    def device(which_plane, place):
        return {"trc": which_plane * HALF + place, "lev": l}

    below, above = {"trc": t, "lev": l - 1}, {"trc": t, "lev": l + 1}

    def put(src, dst, send, recv, to):
        pltpu.make_async_remote_copy(
            src_ref=src, dst_ref=dst, send_sem=send, recv_sem=recv, device_id=to, device_id_type=MESH
        ).start()

    def settle(ref, sem):
        pltpu.make_async_copy(ref, ref, sem).wait()

    def spread(first_k, which_plane, start):
        def one(k, _):
            start(which_plane, lax.rem(me + k, HALF))
            return 0

        lax.fori_loop(first_k, HALF, one, 0)

    loads = [
        pltpu.make_async_copy(fluxes, flux_in, local_sem.at[0]),
        pltpu.make_async_copy(sets, sets_in, local_sem.at[1]),
        pltpu.make_async_copy(steps, steps_in, local_sem.at[2]),
        pltpu.make_async_copy(air_mass, air.at[pl.ds(1, LEV)], local_sem.at[3]),
        pltpu.make_async_copy(tracers, raw.at[pl.ds(1, LEV)], local_sem.at[4]),
        pltpu.make_async_copy(source, source_in.at[pl.ds(0, SETS)], local_sem.at[5]),
    ] + [
        pltpu.make_async_copy(inverse.at[k], matrix.at[:, pl.ds(k * NT, NT)], local_sem.at[6 + k])
        for k in range(SETS)
    ]
    for load in loads:
        load.start()

    barrier = pltpu.get_barrier_semaphore()

    def greet(to):
        pl.semaphore_signal(barrier, inc=1, device_id=to, device_id_type=MESH)

    greet(device(other, me))
    spread(1, plane, lambda which_plane, place: greet(device(which_plane, place)))
    pl.when(has_below)(lambda: greet(below))
    pl.when(has_above)(lambda: greet(above))

    for load in loads[:3]:
        load.wait()
    for level in range(LEV):
        for n in range(3):
            gathered[pl.ds(own + n * LEV + level, 1), :] = flux_in[n, level]
        gathered[pl.ds(own + 12 + level, 1), :] = sets_in[level].astype(F32)
        gathered[pl.ds(own + 16 + level, 1), :] = steps_in[level].astype(F32)
    gathered[pl.ds(own + 20, 4), :] = jnp.zeros((4, LON), F32)

    pl.semaphore_wait(barrier, HALF + has_below.astype(jnp.int32) + has_above.astype(jnp.int32))

    mine = gathered.at[pl.ds(own, 24)]
    short = gathered.at[pl.ds(own, 16)]
    put(mine, mine, flux_send.at[0], flux_recv.at[1], device(other, me))

    @pl.when(has_below)
    def _():
        put(short, pack_above, halo_send.at[0, 0], halo_recv.at[0, 0], below)

    @pl.when(has_above)
    def _():
        put(short, pack_below, halo_send.at[1, 0], halo_recv.at[1, 0], above)

    def share_own(which_plane, place):
        put(mine, mine, flux_send.at[0], flux_recv.at[0], device(which_plane, place))

    spread(1, plane, share_own)

    for load in loads[3:5]:
        load.wait()

    @pl.when(has_below)
    def _():
        put(raw.at[1], raw.at[LEV + 1], halo_send.at[0, 2], halo_recv.at[0, 2], below)
        put(air.at[1], air.at[LEV + 1], halo_send.at[0, 1], halo_recv.at[0, 1], below)

    @pl.when(has_above)
    def _():
        put(raw.at[LEV], raw.at[0], halo_send.at[1, 2], halo_recv.at[1, 2], above)
        put(air.at[LEV], air.at[0], halo_send.at[1, 1], halo_recv.at[1, 1], above)

    def wall(halo, pack):
        raw[halo] = jnp.zeros((TRC, 4, LAT, LON), F32)
        air[halo] = jnp.ones((LAT, LON), F32)
        pack[...] = jnp.zeros((16, LON), F32)

    pl.when(l == 0)(lambda: wall(0, pack_below))
    pl.when(l == 15)(lambda: wall(LEV + 1, pack_above))
    pl.when(has_below)(lambda: settle(pack_below, halo_recv.at[1, 0]))
    pl.when(has_above)(lambda: settle(pack_above, halo_recv.at[0, 0]))

    gathered[pl.ds(own + 24, 8), :] = jnp.concatenate(
        [pack_below[n * LEV + 3 : n * LEV + 4, :] for n in range(3)]
        + [pack_above[n * LEV : n * LEV + 1, :] for n in range(3)]
        + [jnp.zeros((2, LON), F32)],
        axis=0,
    )
    near = gathered.at[pl.ds(own + 24, 8)]
    put(near, near, flux_send.at[0], flux_recv.at[4], device(other, me))

    def share_near(which_plane, place):
        put(near, near, flux_send.at[0], flux_recv.at[2], device(which_plane, place))

    spread(1, plane, share_near)
    settle(gathered.at[pl.ds(0, 15 * 24)], flux_recv.at[0])

    top_level = 16 * LEV - 1
    mid_rows = send_mid.reshape(HALF * 2 * 2 * TRC, LON)
    edge_rows = send_edge.reshape(2 * HALF * 2 * TRC, LON)
    my_rows = pl.ds(pl.multiple_of(t * TRC, TRC), TRC)

    def quick(start, count, keep):
        rows, some = pl.ds(start, count), pl.ds(0, count)
        lane = lax.broadcasted_iota(jnp.int32, (count, LON), 1)
        row = lax.broadcasted_iota(jnp.int32, (count, LON), 0) + start

        def prepare(level, _):
            def flux(direction):
                return gathered[pl.ds(start * PACK + direction * LEV + level, count, stride=PACK), :]

            cell_air = air[1 + level, rows, :]
            upper = jnp.where(lane < LON - 1, flux(0), 0.0)
            new_air, first, _ = coefficients(
                lower_of(cell_air, 1), cell_air, upper_of(cell_air, 1), lower_of(upper, 1), upper
            )
            for n in range(6):
                quick_x[level, n, some] = first[n]
            upper = jnp.where(row < LAT - 1, flux(1), 0.0)
            lower = jnp.where(row > 0, lower_of(upper, 0), 0.0)
            new_air, first, _ = coefficients(
                lower_of(new_air, 0), new_air, upper_of(new_air, 0), lower, upper
            )
            for n in range(6):
                quick_y[level, n, some] = first[n]
            quick_air[level, some] = new_air
            quick_flux[level, some] = flux(2)
            return 0

        lax.fori_loop(0, LEV, prepare, 0)
        for level in (1, 2):
            _, first, _ = coefficients(
                quick_air[level - 1, some], quick_air[level, some], quick_air[level + 1, some],
                quick_flux[level - 1, some], quick_flux[level, some],
            )
            for n in range(6):
                quick_z[level - 1, n, some] = first[n]

        def tracer(n, _):
            mixing, slope = [], []
            for level in range(LEV):
                q, sx, sy, sz = (raw[1 + level, n, f, rows, :] for f in range(4))
                first = [quick_x[level, i, some] for i in range(6)]
                q = carried(means(around(q, 1), around(sx, 1), first), first)
                sy = carried(around(sy, 1), first)
                sz = carried(around(sz, 1), first)
                first = [quick_y[level, i, some] for i in range(6)]
                mixing.append(carried(means(around(q, 0), around(sy, 0), first), first))
                slope.append(carried(around(sz, 0), first))
            for level in (1, 2):
                first = [quick_z[level - 1, i, some] for i in range(6)]
                three = slice(level - 1, level + 2)
                keep(n, level - 1, carried(means(mixing[three], slope[three], first), first))
            return 0

        lax.fori_loop(0, TRC, tracer, 0)

    def keep_own_half(n, level, q):
        mid_rows[pl.ds(plane * 16 + level * TRC + n, HALF, stride=32), :] = q

    quick(pl.multiple_of(plane * HALF, HALF), HALF, keep_own_half)

    def send_own_half(which_plane, place):
        @pl.when(place != edge_row)
        def _():
            put(
                send_mid.at[place, plane], columns.at[pl.ds(1, 2), plane, my_rows],
                cell_send.at[0], cell_recv.at[0], device(which_plane, place),
            )

    spread(0, other, send_own_half)
    spread(1, plane, send_own_half)

    theirs = gathered.at[pl.ds(pl.multiple_of(partner * PACK, PACK), 24)]
    settle(theirs, flux_recv.at[1])

    def share_partner(which_plane, place):
        put(theirs, theirs, flux_send.at[0], flux_recv.at[3], device(which_plane, place))

    spread(1, plane, share_partner)
    settle(gathered.at[pl.ds(0, 15 * 24)], flux_recv.at[3])

    is_low = plane == 0

    def keep_other_half(n, level, q):
        far = jnp.where(is_low, q[HALF:], q[:HALF])
        mid_rows[pl.ds(other * 16 + level * TRC + n, HALF, stride=32), :] = far
        send_row[level, pl.ds(n, 1), :] = jnp.where(is_low, q[HALF - 1 : HALF], q[HALF : HALF + 1])

    quick(0, LAT, keep_other_half)

    def send_other_half(which_plane, place):
        put(
            send_mid.at[place, other], columns.at[pl.ds(1, 2), other, my_rows],
            cell_send.at[0], cell_recv.at[0], device(which_plane, place),
        )

        @pl.when(place == edge_row)
        def _():
            put(
                send_row, columns.at[pl.ds(1, 2), plane, my_rows],
                cell_send.at[0], cell_recv.at[0], device(which_plane, place),
            )

    spread(0, other, send_other_half)
    spread(1, plane, send_other_half)
    columns[pl.ds(1, 2), other, my_rows, :] = send_mid[me, other]
    columns[pl.ds(1, 2), plane, my_rows, :] = jnp.where(
        me == edge_row, send_row[...], send_mid[me, plane]
    )

    their_near = gathered.at[pl.ds(pl.multiple_of(partner * PACK + 24, 8), 8)]
    settle(their_near, flux_recv.at[4])

    def share_their_near(which_plane, place):
        put(their_near, their_near, flux_send.at[0], flux_recv.at[5], device(which_plane, place))

    spread(1, plane, share_their_near)

    lane = lax.broadcasted_iota(jnp.int32, (LAT, LON), 1)
    row = lax.broadcasted_iota(jnp.int32, (LAT, LON), 0)

    def horizontal(level, _):
        def flux(direction):
            inside = direction * LEV + level - 1
            place = jnp.where(level == 0, 24 + direction, jnp.where(level == LEV + 1, 27 + direction, inside))
            return gathered[pl.ds(place, LAT, stride=PACK), :]

        cell_air = air[level]
        upper = jnp.where(lane < LON - 1, flux(0), 0.0)
        new_air, first, second = coefficients(
            lower_of(cell_air, 1), cell_air, upper_of(cell_air, 1), lower_of(upper, 1), upper
        )
        for n in range(6):
            coef[n] = first[n]
            coef[6 + n] = second[n]
        upper = jnp.where(row < LAT - 1, flux(1), 0.0)
        new_air, first, second = coefficients(
            lower_of(new_air, 0), new_air, upper_of(new_air, 0), lower_of(upper, 0), upper
        )
        for n in range(6):
            coef[12 + n] = first[n]
            coef[18 + n] = second[n]
        state[level, 4 * TRC] = new_air
        state[level, 4 * TRC + 1] = jnp.where(l * LEV + level - 1 < top_level, flux(2), 0.0)

        def tracer(n, _):
            q, sx, sy, sz = (raw[level, n, f] for f in range(4))
            first = [coef[i] for i in range(6)]
            second = [coef[6 + i] for i in range(6)]
            slope = around(sx, 1)
            mean = means(around(q, 1), slope, first)
            q, sx = carried(mean, first), new_slope(mean, slope, second)
            sy, sz = carried(around(sy, 1), first), carried(around(sz, 1), first)
            first = [coef[12 + i] for i in range(6)]
            second = [coef[18 + i] for i in range(6)]
            slope = around(sy, 0)
            mean = means(around(q, 0), slope, first)
            state[level, n] = carried(mean, first)
            state[level, TRC + n] = carried(around(sz, 0), first)
            state[level, 2 * TRC + n] = carried(around(sx, 0), first)
            state[level, 3 * TRC + n] = new_slope(mean, slope, second)
            return 0

        lax.fori_loop(0, TRC, tracer, 0)
        return 0

    lax.fori_loop(1, LEV + 1, horizontal, 0)

    def vertical(level):
        at = level + 1
        _, first, second = coefficients(
            state[at - 1, 4 * TRC], state[at, 4 * TRC], state[at + 1, 4 * TRC],
            state[at - 1, 4 * TRC + 1], state[at, 4 * TRC + 1],
        )
        for i in range(6):
            coef_z[i] = first[i]
            coef_z[6 + i] = second[i]

        def tracer(n, _):
            first = [coef_z[i] for i in range(6)]
            second = [coef_z[6 + i] for i in range(6)]

            def three(f):
                return [state[at + k, f * TRC + n] for k in (-1, 0, 1)]

            slope = three(1)
            mean = means(three(0), slope, first)
            out[level, n, 0] = carried(mean, first)
            out[level, n, 3] = new_slope(mean, slope, second)
            out[level, n, 1] = carried(three(2), first)
            out[level, n, 2] = carried(three(3), first)
            return 0

        lax.fori_loop(0, TRC, tracer, 0)

    def inner_level(level, _):
        vertical(level)
        return 0

    lax.fori_loop(1, 3, inner_level, 0)

    settle(gathered.at[pl.ds(0, 15 * 8)], flux_recv.at[2])
    settle(gathered.at[pl.ds(0, 15 * 8)], flux_recv.at[5])

    @pl.when(has_below)
    def _():
        settle(air.at[0], halo_recv.at[1, 1])
        settle(raw.at[0], halo_recv.at[1, 2])

    @pl.when(has_above)
    def _():
        settle(air.at[LEV + 1], halo_recv.at[0, 1])
        settle(raw.at[LEV + 1], halo_recv.at[0, 2])

    def outer_level(i, _):
        return horizontal(i * (LEV + 1), 0)

    lax.fori_loop(0, 2, outer_level, 0)

    def edge_level(which, _):
        level = 3 * which
        vertical(level)

        def keep(n, _):
            for half in range(2):
                edge_rows[pl.ds(which * 256 + half * TRC + n, HALF, stride=16), :] = out[
                    level, n, 0, pl.ds(half * HALF, HALF), :
                ]
            return 0

        lax.fori_loop(0, TRC, keep, 0)

        def send_level(which_plane, place):
            put(
                send_edge.at[which, place], columns.at[level, :, my_rows],
                cell_send.at[1 + which], cell_recv.at[1 + which], device(which_plane, place),
            )

        spread(0, other, send_level)
        spread(1, plane, send_level)
        columns[level, :, my_rows, :] = send_edge[which, me]
        return 0

    lax.fori_loop(0, 2, edge_level, 0)

    for load in loads[5:]:
        load.wait()
    source_in[pl.ds(4, 4), :] = jnp.zeros((4, NT), F32)
    returned_rows = returned.reshape(LEV * 2 * HALF * TRC, LON)

    def assemble(level):
        settle(returned.at[level, :, pl.ds(0, HALF - 1)], back_recv.at[level])

        def tracer(n, _):
            for half in range(2):
                start = level * 256 + half * 128 + n
                out[level, n, 0, pl.ds(half * HALF, HALF), :] = returned_rows[
                    pl.ds(start, HALF, stride=TRC), :
                ]
            return 0

        lax.fori_loop(0, TRC, tracer, 0)

    my_tracers = pl.ds(pl.multiple_of(plane * 128, 128), 128)

    def chemistry(i, _):
        level = jnp.where(i < 2, i + 1, 3 * (i - 2))

        @pl.when(i == 0)
        def _():
            settle(columns.at[pl.ds(1, 2), :, pl.ds(0, 248)], cell_recv.at[0])

        @pl.when(i == 2)
        def _():
            settle(columns.at[0, :, pl.ds(0, 248)], cell_recv.at[1])

        @pl.when(i == 3)
        def _():
            assemble(1)
            assemble(2)
            settle(columns.at[3, :, pl.ds(0, 248)], cell_recv.at[2])

        def cell_row(offset):
            return jnp.concatenate(
                [gathered[pl.ds((half * HALF + me) * PACK + offset + level, 1), :] for half in range(2)], axis=1
            )

        cell_sets, cell_steps = cell_row(12), cell_row(16)
        masks = [(cell_sets == k).astype(F32) for k in range(SETS)]
        by_set = source_in[...].T
        added = masks[0] * by_set[:, 0:1]
        for k in range(1, SETS):
            added = added + masks[k] * by_set[:, k : k + 1]
        masks = [m.astype(jnp.bfloat16) for m in masks]
        work[0] = jnp.concatenate([columns[level, 0], columns[level, 1]], axis=1)
        work[1] = added

        def step(turn, _):
            now = work[0]
            rounded = now.astype(jnp.bfloat16)
            chosen = jnp.concatenate([rounded * m for m in masks], axis=0)
            product = jnp.dot(matrix[...], chosen, preferred_element_type=F32)
            work[0] = jnp.where(turn.astype(F32) < cell_steps, product + work[1], now)
            return 0

        lax.fori_loop(0, NSTEP, step, 0)
        for half in range(2):
            finished[level, half] = work[0, my_tracers, pl.ds(half * LON, LON)]

        def send_back(which_plane, place):
            put(
                finished.at[level, :, pl.ds(pl.multiple_of(place * TRC, TRC), TRC)], returned.at[level, :, me],
                back_send.at[0], back_recv.at[level], device(which_plane, place),
            )

        spread(1, plane, send_back)
        returned[level, :, me] = finished[level, :, pl.ds(pl.multiple_of(me * TRC, TRC), TRC), :]
        return 0

    lax.fori_loop(0, LEV, chemistry, 0)
    assemble(0)
    assemble(3)

    settle(gathered.at[pl.ds(0, 31 * PACK)], flux_send.at[0])

    def halo_sent(side):
        settle(pack_below, halo_send.at[side, 0])
        settle(air.at[0], halo_send.at[side, 1])
        settle(raw.at[0], halo_send.at[side, 2])

    pl.when(has_below)(lambda: halo_sent(0))
    pl.when(has_above)(lambda: halo_sent(1))
    settle(columns.at[pl.ds(1, 2), :, pl.ds(0, 248)], cell_send.at[0])
    settle(columns.at[0, :, pl.ds(0, 248)], cell_send.at[1])
    settle(columns.at[3, :, pl.ds(0, 248)], cell_send.at[2])
    settle(returned.at[:, :, pl.ds(0, HALF - 1)], back_send.at[0])


def on_device(tracers, air_mass, mass_flux, chem_inverse, chem_source, reaction_set, chem_steps):
    hbm = pl.BlockSpec(memory_space=pltpu.HBM)
    dma, vmem = pltpu.SemaphoreType.DMA, pltpu.VMEM
    return pl.pallas_call(
        kernel,
        name="advect_and_react",
        out_shape=pltpu.VMEM(tracers.shape, F32),
        in_specs=[hbm] * 7,
        out_specs=pl.BlockSpec(memory_space=pltpu.VMEM),
        scratch_shapes=[
            vmem((LEV + 2,) + tracers.shape[1:], F32),
            vmem((LEV + 2, LAT, LON), F32),
            vmem(mass_flux.shape, F32),
            vmem(reaction_set.shape, jnp.int32),
            vmem(chem_steps.shape, jnp.int32),
            vmem((NT, SETS * NT), jnp.bfloat16),
            vmem((8, NT), F32),
            vmem((LAT * PACK, LON), F32),
            vmem((16, LON), F32),
            vmem((16, LON), F32),
            vmem((LEV, 6, LAT, LON), F32),
            vmem((LEV, 6, LAT, LON), F32),
            vmem((2, 6, LAT, LON), F32),
            vmem((LEV, LAT, LON), F32),
            vmem((LEV, LAT, LON), F32),
            vmem((24, LAT, LON), F32),
            vmem((12, LAT, LON), F32),
            vmem((LEV + 2, 4 * TRC + 2, LAT, LON), F32),
            vmem((HALF, 2, 2, TRC, LON), F32),
            vmem((2, HALF, 2, TRC, LON), F32),
            vmem((2, TRC, LON), F32),
            vmem((LEV, 2, NT, LON), F32),
            vmem((2, NT, 2 * LON), F32),
            vmem((LEV, 2, NT // 2, LON), F32),
            vmem((LEV, 2, HALF, TRC, LON), F32),
            dma((10,)),
            dma((1,)),
            dma((6,)),
            dma((2, 3)),
            dma((2, 3)),
            dma((3,)),
            dma((3,)),
            dma((1,)),
            dma((LEV,)),
        ],
        compiler_params=pltpu.CompilerParams(
            collective_id=0, has_side_effects=True, vmem_limit_bytes=40 * 1024 * 1024
        ),
    )(
        *(
            pltpu.with_memory_space_constraint(value, pltpu.HBM)
            for value in (
                tracers, air_mass, mass_flux, chem_inverse, chem_source, reaction_set, chem_steps
            )
        )
    )


def solution(mesh):
    return jax.shard_map(
        on_device,
        mesh=mesh,
        in_specs=(
            P("lev", "trc", None, None, None),
            P("lev", None, None),
            P(None, "lev", "trc", None),
            P(),
            P(),
            P("lev", "trc", None),
            P("lev", "trc", None),
        ),
        out_specs=P("lev", "trc", None, None, None),
        check_vma=False,
    )
```

time: 99.6 us -> 83.9 us (0.84)
  the two profiles are of different devices: /device:TPU:64 before, /device:TPU:32 now
where the time goes in v2:
time: 83.9 us; the launch traced here: 83.8 us
  Pallas kernels  82.5 us (98%)
  local copies, waits for them, and re-layouts  1.32 us (2%)
    pallas_call x1, Pallas kernels, on_device(): pl.pallas_call(kernel, name='advect_and_react', out_shape=pltpu.VMEM(trac...  82.5 us

profile of v2, /device:TPU:32, one launch (start us, length us, event | category | flops | bytes accessed | tf_op | source)
XLA Modules:
  0.0 83.8 jit_solution(7481865544987687943)
XLA Ops:
  0.0 82.5 %advect_and_react.1 = f32[4,8,4,32,128]{4,3,2,1,0:T(8,128)S(1)} custom-call(f32[4,8,4,32,128]{4,3,2,1,0:T(8,128)} %tracers.1, f32[4,32,128]{2,1,0:T(8,128)} %air_mass.1, f32[3,4,1,128]{3,2,1,0:T(1,128)} %fluxes.1, bf16[4,256,256]{2,1,0:T(8,128)(2,1)} %inverse.1, f32[4,256]{1,0:T(4,128)} %source.1, s32[4,1,128]{2,1,0:T(1,128)} %sets.1, s32[4,1,128]{2,1,0:T(1,128)} %steps.1), custom_call_target="tpu_custom_call" | custom-call | tf_op jit(solution)/shard_map/advect_and_react/pallas_call | solution.py:541
  82.5 1.3 %copy.9 = f32[4,8,4,32,128]{4,3,2,1,0:T(8,128)} copy(f32[4,8,4,32,128]{4,3,2,1,0:T(8,128)S(1)} %advect_and_react.1) | data formatting | bytes 4194304

commit v3 on v2

--- a/solution.py
+++ b/solution.py
@@ -225,7 +225,7 @@
             quick_flux[level, some] = flux(2)
             return 0
 
-        lax.fori_loop(0, LEV, prepare, 0)
+        lax.fori_loop(0, LEV, prepare, 0, unroll=2 if count == HALF else 1)
         for level in (1, 2):
             _, first, _ = coefficients(
                 quick_air[level - 1, some], quick_air[level, some], quick_air[level + 1, some],
@@ -251,7 +251,7 @@
                 keep(n, level - 1, carried(means(mixing[three], slope[three], first), first))
             return 0
 
-        lax.fori_loop(0, TRC, tracer, 0)
+        lax.fori_loop(0, TRC, tracer, 0, unroll=2 if count == HALF else 1)
 
     def keep_own_half(n, level, q):
         mid_rows[pl.ds(plane * 16 + level * TRC + n, HALF, stride=32), :] = q
@@ -440,6 +440,13 @@
         columns[level, :, my_rows, :] = send_edge[which, me]
         return 0
 
+    pace = lax.div(l, 2)
+    held = (pace == 5) | (pace == 6)
+
+    @pl.when(held)
+    def _():
+        settle(columns.at[pl.ds(1, 2), :, pl.ds(0, 248)], cell_recv.at[0])
+
     lax.fori_loop(0, 2, edge_level, 0)
 
     for load in loads[5:]:
@@ -465,7 +472,7 @@
     def chemistry(i, _):
         level = jnp.where(i < 2, i + 1, 3 * (i - 2))
 
-        @pl.when(i == 0)
+        @pl.when((i == 0) & jnp.logical_not(held))
         def _():
             settle(columns.at[pl.ds(1, 2), :, pl.ds(0, 248)], cell_recv.at[0])
 

time: 83.9 us -> 80.9 us (0.964)
  the two profiles are of different devices: /device:TPU:32 before, /device:TPU:160 now
where the time goes in v3:
time: 80.9 us; the launch traced here: 80.7 us
  Pallas kernels  79.4 us (98%)
  local copies, waits for them, and re-layouts  1.32 us (2%)
    pallas_call x1, Pallas kernels, on_device(): pl.pallas_call(kernel, name='advect_and_react', out_shape=pltpu.VMEM(trac...  79.4 us

profile of v3, /device:TPU:160, one launch (start us, length us, event | category | flops | bytes accessed | tf_op | source)
XLA Modules:
  0.0 80.7 jit_solution(8568839867640695895)
XLA Ops:
  0.0 79.4 %advect_and_react.1 = f32[4,8,4,32,128]{4,3,2,1,0:T(8,128)S(1)} custom-call(f32[4,8,4,32,128]{4,3,2,1,0:T(8,128)} %tracers.1, f32[4,32,128]{2,1,0:T(8,128)} %air_mass.1, f32[3,4,1,128]{3,2,1,0:T(1,128)} %fluxes.1, bf16[4,256,256]{2,1,0:T(8,128)(2,1)} %inverse.1, f32[4,256]{1,0:T(4,128)} %source.1, s32[4,1,128]{2,1,0:T(1,128)} %sets.1, s32[4,1,128]{2,1,0:T(1,128)} %steps.1), custom_call_target="tpu_custom_call" | custom-call | tf_op jit(solution)/shard_map/advect_and_react/pallas_call | solution.py:548
  79.4 1.3 %copy.9 = f32[4,8,4,32,128]{4,3,2,1,0:T(8,128)} copy(f32[4,8,4,32,128]{4,3,2,1,0:T(8,128)S(1)} %advect_and_react.1) | data formatting | bytes 4194304

commit v4 on v3

--- a/solution.py
+++ b/solution.py
@@ -144,11 +144,11 @@
 
     @pl.when(has_below)
     def _():
-        put(short, pack_above, halo_send.at[0, 0], halo_recv.at[0, 0], below)
+        put(short, pack_above.at[pl.ds(0, 16)], halo_send.at[0, 0], halo_recv.at[0, 0], below)
 
     @pl.when(has_above)
     def _():
-        put(short, pack_below, halo_send.at[1, 0], halo_recv.at[1, 0], above)
+        put(short, pack_below.at[pl.ds(0, 16)], halo_send.at[1, 0], halo_recv.at[1, 0], above)
 
     def share_own(which_plane, place):
         put(mine, mine, flux_send.at[0], flux_recv.at[0], device(which_plane, place))
@@ -171,12 +171,12 @@
     def wall(halo, pack):
         raw[halo] = jnp.zeros((TRC, 4, LAT, LON), F32)
         air[halo] = jnp.ones((LAT, LON), F32)
-        pack[...] = jnp.zeros((16, LON), F32)
+        pack[...] = jnp.zeros((24, LON), F32)
 
     pl.when(l == 0)(lambda: wall(0, pack_below))
     pl.when(l == 15)(lambda: wall(LEV + 1, pack_above))
-    pl.when(has_below)(lambda: settle(pack_below, halo_recv.at[1, 0]))
-    pl.when(has_above)(lambda: settle(pack_above, halo_recv.at[0, 0]))
+    pl.when(has_below)(lambda: settle(pack_below.at[pl.ds(0, 16)], halo_recv.at[1, 0]))
+    pl.when(has_above)(lambda: settle(pack_above.at[pl.ds(0, 16)], halo_recv.at[0, 0]))
 
     gathered[pl.ds(own + 24, 8), :] = jnp.concatenate(
         [pack_below[n * LEV + 3 : n * LEV + 4, :] for n in range(3)]
@@ -194,8 +194,8 @@
     settle(gathered.at[pl.ds(0, 15 * 24)], flux_recv.at[0])
 
     top_level = 16 * LEV - 1
-    mid_rows = send_mid.reshape(HALF * 2 * 2 * TRC, LON)
-    edge_rows = send_edge.reshape(2 * HALF * 2 * TRC, LON)
+    mid_rows = send_mid.reshape((HALF + 1) * 2 * 2 * TRC, LON)
+    edge_rows = send_edge.reshape(3 * HALF * 2 * TRC, LON)
     my_rows = pl.ds(pl.multiple_of(t * TRC, TRC), TRC)
 
     def quick(start, count, keep):
@@ -296,7 +296,7 @@
         @pl.when(place == edge_row)
         def _():
             put(
-                send_row, columns.at[pl.ds(1, 2), plane, my_rows],
+                send_row.at[pl.ds(0, 2)], columns.at[pl.ds(1, 2), plane, my_rows],
                 cell_send.at[0], cell_recv.at[0], device(which_plane, place),
             )
 
@@ -304,7 +304,7 @@
     spread(1, plane, send_other_half)
     columns[pl.ds(1, 2), other, my_rows, :] = send_mid[me, other]
     columns[pl.ds(1, 2), plane, my_rows, :] = jnp.where(
-        me == edge_row, send_row[...], send_mid[me, plane]
+        me == edge_row, send_row[pl.ds(0, 2)], send_mid[me, plane]
     )
 
     their_near = gathered.at[pl.ds(pl.multiple_of(partner * PACK + 24, 8), 8)]
@@ -452,7 +452,7 @@
     for load in loads[5:]:
         load.wait()
     source_in[pl.ds(4, 4), :] = jnp.zeros((4, NT), F32)
-    returned_rows = returned.reshape(LEV * 2 * HALF * TRC, LON)
+    returned_rows = returned.reshape((LEV + 1) * 2 * HALF * TRC, LON)
 
     def assemble(level):
         settle(returned.at[level, :, pl.ds(0, HALF - 1)], back_recv.at[level])
@@ -530,7 +530,7 @@
     settle(gathered.at[pl.ds(0, 31 * PACK)], flux_send.at[0])
 
     def halo_sent(side):
-        settle(pack_below, halo_send.at[side, 0])
+        settle(pack_below.at[pl.ds(0, 16)], halo_send.at[side, 0])
         settle(air.at[0], halo_send.at[side, 1])
         settle(raw.at[0], halo_send.at[side, 2])
 
@@ -539,7 +539,7 @@
     settle(columns.at[pl.ds(1, 2), :, pl.ds(0, 248)], cell_send.at[0])
     settle(columns.at[0, :, pl.ds(0, 248)], cell_send.at[1])
     settle(columns.at[3, :, pl.ds(0, 248)], cell_send.at[2])
-    settle(returned.at[:, :, pl.ds(0, HALF - 1)], back_send.at[0])
+    settle(returned.at[pl.ds(0, LEV), :, pl.ds(0, HALF - 1)], back_send.at[0])
 
 
 def on_device(tracers, air_mass, mass_flux, chem_inverse, chem_source, reaction_set, chem_steps):
@@ -559,9 +559,9 @@
             vmem(chem_steps.shape, jnp.int32),
             vmem((NT, SETS * NT), jnp.bfloat16),
             vmem((8, NT), F32),
-            vmem((LAT * PACK, LON), F32),
-            vmem((16, LON), F32),
-            vmem((16, LON), F32),
+            vmem(((LAT + 1) * PACK, LON), F32),
+            vmem((24, LON), F32),
+            vmem((24, LON), F32),
             vmem((LEV, 6, LAT, LON), F32),
             vmem((LEV, 6, LAT, LON), F32),
             vmem((2, 6, LAT, LON), F32),
@@ -570,13 +570,13 @@
             vmem((24, LAT, LON), F32),
             vmem((12, LAT, LON), F32),
             vmem((LEV + 2, 4 * TRC + 2, LAT, LON), F32),
-            vmem((HALF, 2, 2, TRC, LON), F32),
-            vmem((2, HALF, 2, TRC, LON), F32),
-            vmem((2, TRC, LON), F32),
+            vmem((HALF + 1, 2, 2, TRC, LON), F32),
+            vmem((3, HALF, 2, TRC, LON), F32),
+            vmem((3, TRC, LON), F32),
             vmem((LEV, 2, NT, LON), F32),
             vmem((2, NT, 2 * LON), F32),
             vmem((LEV, 2, NT // 2, LON), F32),
-            vmem((LEV, 2, HALF, TRC, LON), F32),
+            vmem((LEV + 1, 2, HALF, TRC, LON), F32),
             dma((10,)),
             dma((1,)),
             dma((6,)),

time: 80.9 us -> 80.9 us (level)
  no operation moved by 1% of the time
where the time goes in v4:
time: 80.9 us; the launch traced here: 80.7 us
  Pallas kernels  79.4 us (98%)
  local copies, waits for them, and re-layouts  1.32 us (2%)
    pallas_call x1, Pallas kernels, on_device(): pl.pallas_call(kernel, name='advect_and_react', out_shape=pltpu.VMEM(trac...  79.4 us

profile of v4, /device:TPU:160, one launch (start us, length us, event | category | flops | bytes accessed | tf_op | source)
XLA Modules:
  0.0 80.7 jit_solution(17128570933771431697)
XLA Ops:
  0.0 79.4 %advect_and_react.1 = f32[4,8,4,32,128]{4,3,2,1,0:T(8,128)S(1)} custom-call(f32[4,8,4,32,128]{4,3,2,1,0:T(8,128)} %tracers.1, f32[4,32,128]{2,1,0:T(8,128)} %air_mass.1, f32[3,4,1,128]{3,2,1,0:T(1,128)} %fluxes.1, bf16[4,256,256]{2,1,0:T(8,128)(2,1)} %inverse.1, f32[4,256]{1,0:T(4,128)} %source.1, s32[4,1,128]{2,1,0:T(1,128)} %sets.1, s32[4,1,128]{2,1,0:T(1,128)} %steps.1), custom_call_target="tpu_custom_call" | custom-call | tf_op jit(solution)/shard_map/advect_and_react/pallas_call | solution.py:548
  79.4 1.3 %copy.9 = f32[4,8,4,32,128]{4,3,2,1,0:T(8,128)} copy(f32[4,8,4,32,128]{4,3,2,1,0:T(8,128)S(1)} %advect_and_react.1) | data formatting | bytes 4194304

commit v5 on v4

--- a/solution.py
+++ b/solution.py
@@ -225,7 +225,7 @@
             quick_flux[level, some] = flux(2)
             return 0
 
-        lax.fori_loop(0, LEV, prepare, 0, unroll=2 if count == HALF else 1)
+        lax.fori_loop(0, LEV, prepare, 0, unroll=4 if count == HALF else 1)
         for level in (1, 2):
             _, first, _ = coefficients(
                 quick_air[level - 1, some], quick_air[level, some], quick_air[level + 1, some],
@@ -251,7 +251,7 @@
                 keep(n, level - 1, carried(means(mixing[three], slope[three], first), first))
             return 0
 
-        lax.fori_loop(0, TRC, tracer, 0, unroll=2 if count == HALF else 1)
+        lax.fori_loop(0, TRC, tracer, 0, unroll=4 if count == HALF else 1)
 
     def keep_own_half(n, level, q):
         mid_rows[pl.ds(plane * 16 + level * TRC + n, HALF, stride=32), :] = q
@@ -472,20 +472,6 @@
     def chemistry(i, _):
         level = jnp.where(i < 2, i + 1, 3 * (i - 2))
 
-        @pl.when((i == 0) & jnp.logical_not(held))
-        def _():
-            settle(columns.at[pl.ds(1, 2), :, pl.ds(0, 248)], cell_recv.at[0])
-
-        @pl.when(i == 2)
-        def _():
-            settle(columns.at[0, :, pl.ds(0, 248)], cell_recv.at[1])
-
-        @pl.when(i == 3)
-        def _():
-            assemble(1)
-            assemble(2)
-            settle(columns.at[3, :, pl.ds(0, 248)], cell_recv.at[2])
-
         def cell_row(offset):
             return jnp.concatenate(
                 [gathered[pl.ds((half * HALF + me) * PACK + offset + level, 1), :] for half in range(2)], axis=1
@@ -498,8 +484,23 @@
         for k in range(1, SETS):
             added = added + masks[k] * by_set[:, k : k + 1]
         masks = [m.astype(jnp.bfloat16) for m in masks]
+        work[1] = added
+
+        @pl.when((i == 0) & jnp.logical_not(held))
+        def _():
+            settle(columns.at[pl.ds(1, 2), :, pl.ds(0, 248)], cell_recv.at[0])
+
+        @pl.when(i == 2)
+        def _():
+            settle(columns.at[0, :, pl.ds(0, 248)], cell_recv.at[1])
+
+        @pl.when(i == 3)
+        def _():
+            assemble(1)
+            assemble(2)
+            settle(columns.at[3, :, pl.ds(0, 248)], cell_recv.at[2])
+
         work[0] = jnp.concatenate([columns[level, 0], columns[level, 1]], axis=1)
-        work[1] = added
 
         def step(turn, _):
             now = work[0]

time: 80.9 us -> 80.5 us (level)
  no operation moved by 1% of the time
where the time goes in v5:
time: 80.5 us; the launch traced here: 80.4 us
  Pallas kernels  79 us (98%)
  local copies, waits for them, and re-layouts  1.32 us (2%)
    pallas_call x1, Pallas kernels, on_device(): pl.pallas_call(kernel, name='advect_and_react', out_shape=pltpu.VMEM(trac...  79 us

profile of v5, /device:TPU:160, one launch (start us, length us, event | category | flops | bytes accessed | tf_op | source)
XLA Modules:
  0.0 80.4 jit_solution(9590489675857460089)
XLA Ops:
  0.0 79.0 %advect_and_react.1 = f32[4,8,4,32,128]{4,3,2,1,0:T(8,128)S(1)} custom-call(f32[4,8,4,32,128]{4,3,2,1,0:T(8,128)} %tracers.1, f32[4,32,128]{2,1,0:T(8,128)} %air_mass.1, f32[3,4,1,128]{3,2,1,0:T(1,128)} %fluxes.1, bf16[4,256,256]{2,1,0:T(8,128)(2,1)} %inverse.1, f32[4,256]{1,0:T(4,128)} %source.1, s32[4,1,128]{2,1,0:T(1,128)} %sets.1, s32[4,1,128]{2,1,0:T(1,128)} %steps.1), custom_call_target="tpu_custom_call" | custom-call | tf_op jit(solution)/shard_map/advect_and_react/pallas_call | solution.py:549
  79.1 1.3 %copy.9 = f32[4,8,4,32,128]{4,3,2,1,0:T(8,128)} copy(f32[4,8,4,32,128]{4,3,2,1,0:T(8,128)S(1)} %advect_and_react.1) | data formatting | bytes 4194304
